TPU v7x, 512 devices: a whole 4x4x16 slice. The times are simulated.
512 devices in a mesh: section: 8 (over y, core), expert: 64 (over x, z).
Axes of the slice: x: 4, y: 4, z: 16, core: 2. Of those that a mesh axis runs over, the one named last changes fastest.
Arguments:
- fwd_input: bfloat16 [8, 1024, 3584], P('section', 'expert'), may hold values from -6 to 6
- fwd_ids: int32 [8, 1024, 2], P('section', 'expert'), may hold values from 0 to 7, all different within a row; in each aligned block of 16 rows (0 to 15, 16 to 31, ..., all dimensions but the last counted through in order) at most 6 rows name the same one
- bwd_input: bfloat16 [8, 1024, 3584], P('section', 'expert'), may hold values from -6 to 6
- bwd_ids: int32 [8, 1024, 2], P('section', 'expert'), may hold values from 0 to 7, all different within a row; in each aligned block of 16 rows (0 to 15, 16 to 31, ..., all dimensions but the last counted through in order) at most 6 rows name the same one
- bwd_cot: bfloat16 [8, 1024, 3584], P('section', 'expert'), may hold values from -6 to 6
- centroids: bfloat16 [8, 8, 3584], P('section'), may hold values from -0.09375 to 0.09375
- w_gate: bfloat16 [8, 3584, 8192], P('section', None, 'expert'), may hold values from -0.09375 to 0.09375
- w_up: bfloat16 [8, 3584, 8192], P('section', None, 'expert'), may hold values from -0.09375 to 0.09375
- w_down: bfloat16 [8, 8192, 3584], P('section', 'expert'), may hold values from -0.1875 to 0.1875
Outputs:
- fwd_out: bfloat16 [8, 1024, 3584], P('section', 'expert')
- bwd_out: bfloat16 [8, 1024, 3584], P('section', 'expert')
Inputs may be any that keep to these rules, and one draw needn't show every extreme that they name: `fwd_ids`: each row names 2 different experts. Among the 16 rows of one device at one layer, at most 6 name the same expert, a bound that some block reaches in every draw. `bwd_ids`: as fwd_ids.
All inputs are finite; a program needn't handle non-finite values.
Results may differ from a plain program's by a relative error of at most 0.0075.
Values may be sent and summed in bfloat16 or wider, within the bound.
A program may use at most 64 MiB of HBM per device.

v0:
```python
import jax
import jax.numpy as jnp
from jax import lax
from jax.sharding import PartitionSpec as P

EF = 8
CAP = 6


EPS = 1e-06
ROUTE_SCALE = 2.5


def from_behind(block, axis, distance):
    devices = range(lax.axis_size(axis))
    route = [((i - distance) % len(devices), i) for i in devices]
    return lax.ppermute(block, axis, route)


def normalize_rows(values):
    widened = values.astype(jnp.float32)
    inverse = lax.rsqrt(jnp.mean(widened * widened, axis=-1, keepdims=True) + EPS)
    return (widened, inverse, (widened * inverse).astype(jnp.bfloat16))


def router_gates(normed, route_ids, centre_w):
    logits = lax.dot_general(
        normed, centre_w, (((1,), (1,)), ((), ())), preferred_element_type=jnp.float32
    )
    chosen_hot = (route_ids[..., None] == jnp.arange(EF, dtype=jnp.int32)).astype(jnp.float32)
    chosen = jnp.sum(chosen_hot * logits[:, None, :], axis=-1)
    affinity = jax.nn.sigmoid(chosen)
    affinity_sum = jnp.sum(affinity, axis=-1, keepdims=True)
    return (chosen_hot, affinity, affinity_sum, affinity / affinity_sum)


def slot_table_of(route_ids):
    flat_ids = route_ids.reshape(-1)
    slot_hits = (flat_ids[:, None] == jnp.arange(EF, dtype=jnp.int32)).astype(jnp.int32)
    earlier = jnp.cumsum(slot_hits, axis=0, dtype=jnp.int32) - slot_hits
    slot_index = jnp.sum(earlier * slot_hits, axis=-1, dtype=jnp.int32)
    places = (flat_ids * CAP + slot_index).reshape(route_ids.shape)
    return (places[..., None] == jnp.arange(EF * CAP, dtype=jnp.int32)).astype(jnp.float32)


def spread_rows(slot_table, values, shards):
    flat_table = jnp.sum(slot_table, axis=1).astype(jnp.bfloat16)
    gathered = lax.dot_general(
        flat_table, values, (((0,), (0,)), ((), ())), preferred_element_type=jnp.float32
    )
    gathered = gathered.astype(jnp.bfloat16).reshape(EF, 1, CAP, values.shape[-1])
    return jnp.broadcast_to(gathered, (EF, shards, CAP, values.shape[-1])).reshape(
        EF * shards, CAP, values.shape[-1]
    )


def contract_cols(left, right):
    return lax.dot_general(
        left, right, (((1,), (1,)), ((), ())), preferred_element_type=jnp.float32
    )


def forward_rows(in_rows, gate_w, up_w, down_w):
    gate_pre = jnp.dot(in_rows, gate_w, preferred_element_type=jnp.float32)
    up_pre = jnp.dot(in_rows, up_w, preferred_element_type=jnp.float32)
    hidden_act = (gate_pre * jax.nn.sigmoid(gate_pre) * up_pre).astype(jnp.bfloat16)
    return jnp.dot(hidden_act, down_w, preferred_element_type=jnp.float32).astype(jnp.bfloat16)


def backward_rows(in_rows, grad_rows, gate_w, up_w, down_w):
    gate_pre = jnp.dot(in_rows, gate_w, preferred_element_type=jnp.float32)
    up_pre = jnp.dot(in_rows, up_w, preferred_element_type=jnp.float32)
    gate_sig = jax.nn.sigmoid(gate_pre)
    hidden_act = (gate_pre * gate_sig * up_pre).astype(jnp.bfloat16)
    grad_act = contract_cols(grad_rows, down_w)
    dot_rows = jnp.sum(hidden_act.astype(jnp.float32) * grad_act, axis=-1).astype(jnp.bfloat16)
    grad_gate = (grad_act * up_pre * gate_sig * (1.0 + gate_pre * (1.0 - gate_sig))).astype(
        jnp.bfloat16
    )
    grad_up = (grad_act * gate_pre * gate_sig).astype(jnp.bfloat16)
    grad_in = contract_cols(grad_gate, gate_w) + contract_cols(grad_up, up_w)
    return (grad_in.astype(jnp.bfloat16), dot_rows)


def on_device(fwd_input, fwd_ids, bwd_input, bwd_ids, bwd_cot, centroids, w_gate, w_up, w_down):
    experts = lax.axis_size("expert")
    shards = experts // EF
    gate_w = w_gate[0]
    up_w = w_up[0]
    down_w = w_down[0]
    centre_w = centroids[0]
    feature_width = fwd_input.shape[-1]
    carried = from_behind(fwd_input, "section", 1)[0]
    plain_fwd, inverse_fwd, normed_fwd = normalize_rows(carried)
    hot_fwd, affinity_fwd, denom_fwd, share_fwd = router_gates(normed_fwd, fwd_ids[0], centre_w)
    table_fwd = slot_table_of(fwd_ids[0])
    sent_fwd = spread_rows(table_fwd, normed_fwd, shards)
    cotangent = bwd_cot[0]
    plain_bwd, inverse_bwd, normed_bwd = normalize_rows(bwd_input[0])
    hot_bwd, affinity_bwd, denom_bwd, share_bwd = router_gates(normed_bwd, bwd_ids[0], centre_w)
    table_bwd = slot_table_of(bwd_ids[0])
    sent_normed = spread_rows(table_bwd, normed_bwd, shards)
    sent_grads = spread_rows(table_bwd, cotangent, shards)
    received = lax.all_to_all(sent_fwd, "expert", split_axis=0, concat_axis=0, tiled=True)
    result_fwd = forward_rows(received.reshape(-1, feature_width), gate_w, up_w, down_w).reshape(
        received.shape
    )
    back_fwd = lax.all_to_all(result_fwd, "expert", split_axis=0, concat_axis=0, tiled=True)
    rows_normed = lax.all_to_all(sent_normed, "expert", split_axis=0, concat_axis=0, tiled=True)
    rows_grads = lax.all_to_all(sent_grads, "expert", split_axis=0, concat_axis=0, tiled=True)
    grad_in, dot_rows = backward_rows(
        rows_normed.reshape(-1, feature_width),
        rows_grads.reshape(-1, feature_width),
        gate_w,
        up_w,
        down_w,
    )
    back_grads = lax.all_to_all(
        grad_in.reshape(rows_normed.shape), "expert", split_axis=0, concat_axis=0, tiled=True
    )
    back_dots = lax.all_to_all(
        dot_rows.reshape(rows_normed.shape[:2]), "expert", split_axis=0, concat_axis=0, tiled=True
    )
    summed_fwd = jnp.sum(
        back_fwd.reshape(EF, shards, CAP, feature_width), axis=1, dtype=jnp.float32
    ).reshape(EF * CAP, feature_width)
    mixing_fwd = jnp.sum(ROUTE_SCALE * share_fwd[..., None] * table_fwd, axis=1)
    routed = jnp.dot(mixing_fwd, summed_fwd, precision=lax.Precision.HIGHEST)
    fwd_out = (plain_fwd + routed).astype(jnp.bfloat16)[None]
    summed_grads = jnp.sum(
        back_grads.reshape(EF, shards, CAP, feature_width), axis=1, dtype=jnp.float32
    ).reshape(EF * CAP, feature_width)
    dot_sums = jnp.sum(back_dots.reshape(EF, shards, CAP), axis=1, dtype=jnp.float32).reshape(
        EF * CAP
    )
    gate_dots = jnp.einsum("tkq,q->tk", table_bwd, dot_sums, precision=lax.Precision.HIGHEST)
    scaled = ROUTE_SCALE * gate_dots
    centre = jnp.sum(share_bwd * scaled, axis=-1, keepdims=True)
    gate_slope = (scaled - centre) / denom_bwd * affinity_bwd * (1.0 - affinity_bwd)
    mixing_bwd = jnp.sum(ROUTE_SCALE * share_bwd[..., None] * table_bwd, axis=1)
    grad_normed = jnp.dot(mixing_bwd, summed_grads, precision=lax.Precision.HIGHEST)
    slope_full = jnp.sum(gate_slope[..., None] * hot_bwd, axis=1)
    grad_normed = grad_normed + jnp.dot(
        slope_full, centre_w.astype(jnp.float32), precision=lax.Precision.HIGHEST
    )
    projection = jnp.mean(grad_normed * plain_bwd, axis=-1, keepdims=True)
    result = (
        cotangent.astype(jnp.float32)
        + inverse_bwd * grad_normed
        - inverse_bwd * inverse_bwd * inverse_bwd * plain_bwd * projection
    )
    bwd_out = result.astype(jnp.bfloat16)[None]
    return (fwd_out, bwd_out)


def solution(mesh):
    return jax.shard_map(
        on_device,
        mesh=mesh,
        in_specs=(
            P("section", "expert", None),
            P("section", "expert", None),
            P("section", "expert", None),
            P("section", "expert", None),
            P("section", "expert", None),
            P("section", None, None),
            P("section", None, "expert"),
            P("section", None, "expert"),
            P("section", "expert", None),
        ),
        out_specs=(P("section", "expert", None), P("section", "expert", None)),
        check_vma=False,
    )
```

profile of v0, /device:TPU:24, one launch (start us, length us, event | category | flops | bytes accessed | tf_op | source)
XLA Modules:
  0.0 923.3 jit_solution(2414931868861678358)
XLA Ops:
  0.6 1.1 fusion.27
  1.8 0.6 multiply_multiply_fusion
  2.4 0.8 copy.71
  3.1 1.1 fusion.40
  4.2 0.7 select_reduce_fusion.5
  4.9 0.5 fusion.70
  5.5 0.5 copy-done.10
  6.0 0.5 broadcast_multiply_fusion
  7.1 0.7 multiply_add_fusion
  7.9 1.2 convolution_convert_fusion.1
  9.2 2.1 broadcast_in_dim.22
  11.3 18.9 %all-to-all-start.3 = ((bf16[64,6,3584]{2,1,0:T(8,128)(2,1)}), bf16[64,6,3584]{2,1,0:T(8,128)(2,1)}, u32[]{:S(2)}, u32[]{:S(2)}) async-start(bf16[64,6,3584]{2,1,0:T(8,128)(2,1)} %bitcast.118), calls=%async_computation.3 | async-start | bytes 7340032 | tf_op jit(solution)/shard_map/all_to_all | solution.py:109
  30.2 0.3 convolution_convert_fusion.2
  30.6 165.1 %all-to-all-done.3 = bf16[64,6,3584]{2,1,0:T(8,128)(2,1)} async-done(((bf16[64,6,3584]{2,1,0:T(8,128)(2,1)}), bf16[64,6,3584]{2,1,0:T(8,128)(2,1)}, u32[]{:S(2)}, u32[]{:S(2)}) %all-to-all-start.3) | async-done | bytes 2752544 | tf_op jit(solution)/shard_map/all_to_all | solution.py:109
  195.7 2.2 broadcast_in_dim.20
  197.9 7.7 all-to-all-start.2
  206.4 3.5 collective-permute-done
  210.3 0.7 convert_reduce_fusion.3
  211.0 5.6 reshape.197
  216.6 2.8 fusion.14
  219.4 0.9 fusion.8
  220.3 150.6 %all-to-all-done.2 = bf16[64,6,3584]{2,1,0:T(8,128)(2,1)} async-done(((bf16[64,6,3584]{2,1,0:T(8,128)(2,1)}), bf16[64,6,3584]{2,1,0:T(8,128)(2,1)}, u32[]{:S(2)}, u32[]{:S(2)}) %all-to-all-start.2) | async-done | bytes 2752544 | tf_op jit(solution)/shard_map/all_to_all | solution.py:110
  370.9 5.5 reshape.195
  376.4 3.0 multiply_reduce_fusion
  379.3 0.8 convert_element_type.174
  380.1 7.3 all-to-all-start.5
  387.5 0.3 convolution_convert_fusion.3
  387.9 13.9 %all-to-all-done.5 = bf16[64,1,6]{2,1,0:T(2,128)(2,1)S(1)} async-done(((bf16[64,1,6]{2,1,0:T(2,128)(2,1)}), bf16[64,1,6]{2,1,0:T(2,128)(2,1)S(1)}, u32[]{:S(2)}, u32[]{:S(2)}) %all-to-all-start.5) | async-done | bytes 800 | tf_op jit(solution)/shard_map/all_to_all | solution.py:121
  401.8 2.1 broadcast_in_dim.17
  403.9 5.6 all-to-all-start
  409.5 0.9 fusion.12
  410.4 2.5 fusion
  412.9 5.5 reshape.198
  418.4 154.9 %all-to-all-done = bf16[64,6,3584]{2,1,0:T(8,128)(2,1)} async-done(((bf16[64,6,3584]{2,1,0:T(8,128)(2,1)}), bf16[64,6,3584]{2,1,0:T(8,128)(2,1)}, u32[]{:S(2)}, u32[]{:S(2)}) %all-to-all-start) | async-done | bytes 2752544 | tf_op jit(solution)/shard_map/all_to_all | solution.py:104
  573.3 8.0 all-to-all-start.4
  581.3 5.5 reshape.191
  586.8 2.7 fusion.16
  589.5 6.3 convolution_convert_fusion
  595.9 5.4 reshape.192
  601.3 145.1 %all-to-all-done.4 = bf16[64,6,3584]{2,1,0:T(8,128)(2,1)} async-done(((bf16[64,6,3584]{2,1,0:T(8,128)(2,1)}), bf16[64,6,3584]{2,1,0:T(8,128)(2,1)}, u32[]{:S(2)}, u32[]{:S(2)}) %all-to-all-start.4) | async-done | bytes 2752544 | tf_op jit(solution)/shard_map/all_to_all | solution.py:118
  746.4 7.6 all-to-all-start.1
  754.6 2.9 convert_reduce_fusion
  757.5 0.4 fusion.71
  758.0 0.4 fusion.32
  758.4 0.8 fusion.42
  759.2 160.0 %all-to-all-done.1 = bf16[64,6,3584]{2,1,0:T(8,128)(2,1)} async-done(((bf16[64,6,3584]{2,1,0:T(8,128)(2,1)}), bf16[64,6,3584]{2,1,0:T(8,128)(2,1)}, u32[]{:S(2)}, u32[]{:S(2)}) %all-to-all-start.1) | async-done | bytes 2752544 | tf_op jit(solution)/shard_map/all_to_all | solution.py:108
  919.2 2.9 convert_reduce_fusion.1
  922.2 1.1 fusion.2
  (74 shorter events, 2.8 us)
Async XLA Ops:
  0.6 218.8 %copy-start = (bf16[1,3584,128]{2,1,0:T(8,128)(2,1)S(1)}, bf16[1,3584,128]{2,1,0:T(8,128)(2,1)}, u32[]{:S(2)}) copy-start(bf16[1,3584,128]{2,1,0:T(8,128)(2,1)} %param.16) | copy-start | bytes 2752516
  2.4 5.5 copy-start.16
  5.5 0.5 copy-start.10
  7.8 3.5 copy-start.12
  11.3 18.9 %copy-start.5 = (bf16[1,16,3584]{2,1,0:T(8,128)(2,1)S(1)}, bf16[1,16,3584]{2,1,0:T(8,128)(2,1)}, u32[]{:S(2)}) copy-start(bf16[1,16,3584]{2,1,0:T(8,128)(2,1)} %param.13) | copy-start | bytes 344068
  11.3 184.4 %all-to-all-start.3 = ((bf16[64,6,3584]{2,1,0:T(8,128)(2,1)}), bf16[64,6,3584]{2,1,0:T(8,128)(2,1)}, u32[]{:S(2)}, u32[]{:S(2)}) async-start(bf16[64,6,3584]{2,1,0:T(8,128)(2,1)} %bitcast.118), calls=%async_computation.3 | async-start | bytes 7340032 | tf_op jit(solution)/shard_map/all_to_all | solution.py:109
  197.9 7.8 copy-start.19
  197.9 7.8 copy-start.9
  197.9 12.1 %copy-start.6 = (bf16[1,8,3584]{2,1,0:T(8,128)(2,1)S(1)}, bf16[1,8,3584]{2,1,0:T(8,128)(2,1)}, u32[]{:S(2)}) copy-start(bf16[1,8,3584]{2,1,0:T(8,128)(2,1)} %param.14) | copy-start | bytes 172036
  197.9 173.0 %all-to-all-start.2 = ((bf16[64,6,3584]{2,1,0:T(8,128)(2,1)}), bf16[64,6,3584]{2,1,0:T(8,128)(2,1)}, u32[]{:S(2)}, u32[]{:S(2)}) async-start(bf16[64,6,3584]{2,1,0:T(8,128)(2,1)} %bitcast.116), calls=%async_computation.2 | async-start | bytes 7340032 | tf_op jit(solution)/shard_map/all_to_all | solution.py:110
  205.7 4.2 collective-permute-start
  211.0 5.6 copy-start.2
  216.6 2.8 copy-start.1
  380.1 21.7 %all-to-all-start.5 = ((bf16[64,1,6]{2,1,0:T(2,128)(2,1)}), bf16[64,1,6]{2,1,0:T(2,128)(2,1)S(1)}, u32[]{:S(2)}, u32[]{:S(2)}) async-start(bf16[64,1,6]{2,1,0:T(2,128)(2,1)} %convert_element_type.174), calls=%async_computation.5 | async-start | bytes 65536 | tf_op jit(solution)/shard_map/all_to_all | solution.py:121
  403.9 169.4 %all-to-all-start = ((bf16[64,6,3584]{2,1,0:T(8,128)(2,1)}), bf16[64,6,3584]{2,1,0:T(8,128)(2,1)}, u32[]{:S(2)}, u32[]{:S(2)}) async-start(bf16[64,6,3584]{2,1,0:T(8,128)(2,1)} %bitcast.117), calls=%async_computation | async-start | bytes 7340032 | tf_op jit(solution)/shard_map/all_to_all | solution.py:104
  573.3 173.1 %all-to-all-start.4 = ((bf16[64,6,3584]{2,1,0:T(8,128)(2,1)}), bf16[64,6,3584]{2,1,0:T(8,128)(2,1)}, u32[]{:S(2)}, u32[]{:S(2)}) async-start(bf16[64,6,3584]{2,1,0:T(8,128)(2,1)} %reshape.198), calls=%async_computation.4 | async-start | bytes 7340032 | tf_op jit(solution)/shard_map/all_to_all | solution.py:118
  586.8 2.7 copy-start.4
  601.3 152.9 %copy-start.13 = (s32[16,2]{0,1:T(2,128)S(1)}, s32[16,2]{0,1:T(2,128)}, u32[]{:S(2)}) copy-start(s32[16,2]{0,1:T(2,128)} %copy-done.12) | copy-start | bytes 388
  601.3 153.1 %copy-start.14 = (f32[16,2]{0,1:T(2,128)S(1)}, f32[16,2]{0,1:T(2,128)}, u32[]{:S(2)}) copy-start(f32[16,2]{0,1:T(2,128)} %get-tuple-element.7) | copy-start | bytes 388
  601.3 153.2 %copy-start.11 = (f32[16]{0:T(128)S(1)}, f32[16]{0:T(128)}, u32[]{:S(2)}) copy-start(f32[16]{0:T(128)} %copy-done.10) | copy-start | bytes 196
  601.3 153.2 %copy-start.15 = (f32[16,2]{0,1:T(2,128)S(1)}, f32[16,2]{0,1:T(2,128)}, u32[]{:S(2)}) copy-start(f32[16,2]{0,1:T(2,128)} %get-tuple-element.9) | copy-start | bytes 388
  601.3 153.2 %copy-start.8 = (s32[1,16,2]{1,2,0:T(2,128)S(1)}, s32[1,16,2]{1,2,0:T(2,128)}, u32[]{:S(2)}) copy-start(s32[1,16,2]{1,2,0:T(2,128)} %param.12) | copy-start | bytes 388
  746.4 172.8 %all-to-all-start.1 = ((bf16[64,6,3584]{2,1,0:T(8,128)(2,1)}), bf16[64,6,3584]{2,1,0:T(8,128)(2,1)}, u32[]{:S(2)}, u32[]{:S(2)}) async-start(bf16[64,6,3584]{2,1,0:T(8,128)(2,1)} %reshape.192), calls=%async_computation.1 | async-start | bytes 7340032 | tf_op jit(solution)/shard_map/all_to_all | solution.py:108
  754.5 3.5 copy-start.3
  754.5 3.9 copy-start.17
  754.5 3.9 copy-start.18
  759.2 163.0 %copy-start.7 = (f32[16,48]{1,0:T(8,128)S(1)}, f32[16,48]{1,0:T(8,128)}, u32[]{:S(2)}) copy-start(f32[16,48]{1,0:T(8,128)} %get-tuple-element.5) | copy-start | bytes 9220
where the time goes:
time: 925 us; the launch traced here: 923 us
  waiting for transfers between devices  793 us (86%)
  starting transfers between devices  55.3 us (6%)
  local copies, waits for them, and re-layouts  37.1 us (4%)
  matrix products  24.3 us (3%)
  other arithmetic  12.5 us (1%)
    all_to_all x1, waiting for transfers between devices, on_device(): lax.all_to_all(sent_normed, 'expert', split_axis=0, concat_axis=0, tiled=...  165 us
    all_to_all x1, waiting for transfers between devices, on_device(): lax.all_to_all(result_fwd, 'expert', split_axis=0, concat_axis=0, tiled=T...  160 us
    all_to_all x1, waiting for transfers between devices, on_device(): lax.all_to_all(sent_fwd, 'expert', split_axis=0, concat_axis=0, tiled=True)  155 us
    all_to_all x1, waiting for transfers between devices, on_device(): lax.all_to_all(sent_grads, 'expert', split_axis=0, concat_axis=0, tiled=T...  151 us
    all_to_all x1, waiting for transfers between devices, on_device(): lax.all_to_all(grad_in.reshape(rows_normed.shape), 'expert', split_axis=0...  145 us
    all_to_all x1, starting transfers between devices, on_device(): lax.all_to_all(sent_normed, 'expert', split_axis=0, concat_axis=0, tiled=...  18.9 us
  transfers between devices with their start and end apart: 7, of which 7 were waited for; matrix products, arithmetic and copies ran while one was open for 5% of the time, Pallas kernels for 0%

commit v1 on v0

v1 whole, which is shorter than its diff:
```python
import functools

import jax
import jax.numpy as jnp
from jax import lax
from jax.experimental import pallas as pl
from jax.experimental.pallas import tpu as pltpu
from jax.sharding import PartitionSpec as P

MESH = pl.DeviceIdType.MESH
EF = 8
CAP = 6
NX = 4
NZ = 16
TOK = 16
EPS = 1e-06
ROUTE_SCALE = 2.5
NC = 2
GROUP = NZ // 2
SLOTS = GROUP * CAP
ROWS = NX * SLOTS
GT = GROUP * TOK
LANES = 128
STEP = 256
DEPTH = 512
F32 = jnp.float32
BF16 = jnp.bfloat16
NT = (((1,), (1,)), ((), ()))


def dot(a, b):
    return jnp.dot(a, b, preferred_element_type=F32)


def dot_nt(a, b):
    return lax.dot_general(a, b, NT, preferred_element_type=F32)


def sigmoid(v):
    return jax.nn.sigmoid(v)


def kernel(
    fx_ref, fid_ref, bx_ref, bid_ref, dy_ref, cent_ref, wg_ref, wu_ref, wd_ref,
    outf_ref, outb_ref,
    wgu, wdv, cpad, rx, zm, zb, tt, tu, thi, tlo, xs, xr, yr, ys, ypr, yps, pacc, pp, rss, rsr, rps, rpr, uvb,
    wsem, shs, shr, zms, zmr, zs, zr, xss, xrs, yss, yrs, ypss, yprs, rsss, rsrs, rpss, rprs,
):
    D = fx_ref.shape[-1]
    DC = D // NC
    FF = wdv.shape[0]
    sec = lax.axis_index("section")
    nsec = lax.axis_size("section")
    pos_e = lax.axis_index("expert")
    x = pos_e // NZ
    z = lax.rem(pos_e, NZ)
    half = z // GROUP

    def dev(dx, dz, ds=0):
        xx = lax.rem(x + dx + NX, NX)
        zz = lax.rem(z + dz + NZ, NZ)
        return (lax.rem(sec + ds + nsec, nsec), xx * NZ + zz)

    def remote(src, dst, ss, rs, device):
        return pltpu.make_async_remote_copy(
            src_ref=src, dst_ref=dst, send_sem=ss, recv_sem=rs, device_id=device, device_id_type=MESH
        )

    barrier = pltpu.get_barrier_semaphore()
    partners = [dev(0, 1), dev(0, -1), dev(1, 0), dev(2, 0), dev(3, 0), dev(0, 0, 1), dev(0, 0, -1)]
    for partner in partners:
        pl.semaphore_signal(barrier, inc=1, device_id=partner, device_id_type=MESH)

    loads = [
        pltpu.make_async_copy(wg_ref, wgu.at[:, pl.ds(0, FF)], wsem.at[0]),
        pltpu.make_async_copy(wu_ref, wgu.at[:, pl.ds(FF, FF)], wsem.at[1]),
        pltpu.make_async_copy(wd_ref, wdv, wsem.at[2]),
    ]
    for load in loads:
        load.start()

    lane16 = lax.broadcasted_iota(jnp.int32, (TOK, LANES), 1)
    chosen = (lane16 == bid_ref[:, 0:1]) | (lane16 == bid_ref[:, 1:2])
    chosen = chosen | (lane16 == fid_ref[:, 0:1] + EF) | (lane16 == fid_ref[:, 1:2] + EF)
    zm[0] = jnp.where(chosen, 1.0, 0.0).astype(BF16)

    def normalize(v):
        wide = v.astype(F32)
        inv = lax.rsqrt(jnp.sum(wide * wide, axis=-1, keepdims=True) * (1.0 / D) + EPS)
        return wide, inv, (wide * inv).astype(BF16)

    _, _, hb = normalize(bx_ref[...])
    for c in range(NC):
        zb[0, c, 0] = hb[:, c * DC : (c + 1) * DC]
        zb[1, c, 0] = dy_ref[:, c * DC : (c + 1) * DC]

    pl.semaphore_wait(barrier, len(partners))

    def z_copy(a, c, slot):
        src = 0 if slot <= 2 else slot - 2
        target = dev(0, 1) if slot % 2 == 1 else dev(0, -1)
        if a < 0:
            return remote(zm.at[src], zm.at[slot], zms.at[slot - 1], zmr.at[slot - 1], target)
        return remote(zb.at[a, c, src], zb.at[a, c, slot], zs.at[a, c, slot - 1], zr.at[a, c, slot - 1], target)

    def pieces(a):
        return [(-1, 0), (0, 0), (0, 1)] if a == 0 else [(a, c) for c in range(NC)]

    def z_start(a):
        for piece in pieces(a):
            for slot in (1, 2):
                z_copy(*piece, slot).start()

    def z_step(a, k):
        for piece in pieces(a):
            for slot in (2 * k - 1, 2 * k):
                if slot < NZ:
                    z_copy(*piece, slot).wait_recv()
                    if slot + 2 < NZ:
                        z_copy(*piece, slot + 2).start()

    z_start(0)
    shift = remote(fx_ref, rx, shs, shr, dev(0, 0, 1))
    shift.start()

    cpad[...] = jnp.zeros_like(cpad)
    cpad[pl.ds(0, 2 * EF), :] = jnp.concatenate([cent_ref[...], cent_ref[...]], axis=0)
    for st in range(2 * NC):
        for gam in range(2):
            yr[st, gam, pl.ds(ROWS, 256 - ROWS), :] = jnp.zeros((256 - ROWS, DC), BF16)
    for gam in range(2):
        ypr[gam, pl.ds(ROWS, 256 - ROWS), :] = jnp.zeros((256 - ROWS, LANES), BF16)

    lane = lax.broadcasted_iota(jnp.int32, (GT, LANES), 1)

    def table(ab, gam):
        mask = zm[pl.ds(GROUP * gam, GROUP)].reshape(GT, LANES)
        row_i = lax.broadcasted_iota(jnp.int32, (GT, GT), 0)
        col_i = lax.broadcasted_iota(jnp.int32, (GT, GT), 1)
        below = jnp.where((row_i // TOK == col_i // TOK) & (col_i < row_i), 1.0, 0.0).astype(BF16)
        place = dot(below, mask)
        maskf = mask.astype(F32)
        base = (lax.broadcasted_iota(jnp.int32, (GT, 1), 0) // TOK * CAP).astype(F32)
        wide_lane = lax.broadcasted_iota(jnp.int32, (GT, 256), 1).astype(F32)
        total = jnp.zeros((GT, 256), F32)
        for d in range(NX):
            expert = 2 * lax.rem(x + d, NX) + half + EF * ab
            pick = lane == expert
            named = jnp.sum(jnp.where(pick, maskf, 0.0), axis=1, keepdims=True)
            slot = jnp.sum(jnp.where(pick, place, 0.0), axis=1, keepdims=True) + base + float(SLOTS * d)
            total = total + jnp.where(wide_lane == slot, named, 0.0)
        tu[ab, gam] = total.astype(BF16)
        tt[ab, gam] = total.T[:ROWS].astype(BF16)

    def gates_of(logits, mask, ab, width):
        inside = (width >= EF * ab) & (width < EF * (ab + 1)) & (mask > 0)
        aff = sigmoid(logits)
        picked = jnp.where(inside, aff, 0.0)
        denom = jnp.sum(picked, axis=1, keepdims=True)
        return inside, aff, denom, picked / denom

    def gates(ab, gam):
        a = 2 * ab
        acc = jnp.zeros((GT, LANES), F32)
        for c in range(NC):
            def add(k, acc, c=c):
                col = pl.multiple_of(k * STEP, STEP)
                rows = zb[a, c, pl.ds(GROUP * gam, GROUP), :, pl.ds(col, STEP)].reshape(GT, STEP)
                return acc + dot_nt(rows, cpad[:, pl.ds(c * DC + col, STEP)])
            acc = lax.fori_loop(0, DC // STEP, add, acc)
        mask = zm[pl.ds(GROUP * gam, GROUP)].reshape(GT, LANES).astype(F32)
        _, _, _, share = gates_of(acc, mask, ab, lane)
        block = lax.broadcasted_iota(jnp.int32, (GT, 256), 1) // SLOTS
        spread = jnp.zeros((GT, 256), F32)
        for d in range(NX):
            expert = 2 * lax.rem(x + d, NX) + half + EF * ab
            g = jnp.sum(jnp.where(lane == expert, share, 0.0), axis=1, keepdims=True)
            spread = jnp.where(block == d, g, spread)
        full = tu[ab, gam].astype(F32) * spread
        high = full.astype(BF16)
        thi[ab, gam] = high
        tlo[ab, gam] = (full - high.astype(F32)).astype(BF16)

    def x_copy(a, gam, d):
        return remote(
            xs.at[a, gam, d - 1], xr.at[a, gam, d], xss.at[a, gam, d - 1], xrs.at[a, gam, d - 1], dev(d, 0)
        )

    def select(a, gam):
        ab = a // 2
        for c in range(NC):
            @pl.loop(0, DC // STEP)
            def _(n, c=c):
                col = pl.multiple_of(n * STEP, STEP)
                rows = zb[a, c, pl.ds(GROUP * gam, GROUP), :, pl.ds(col, STEP)].reshape(GT, STEP)
                got = dot(tt[ab, gam], rows).astype(BF16)
                out = pl.ds(c * DC + col, STEP)
                xr[a, gam, 0, :, out] = got[:SLOTS]
                for d in range(1, NX):
                    xs[a, gam, d - 1, :, out] = got[SLOTS * d : SLOTS * (d + 1)]
        for d in (2, 1, 3):
            x_copy(a, gam, d).start()

    def x_wait(a, gam):
        for d in range(1, NX):
            x_copy(a, gam, d).wait_recv()

    def products(a, gam):
        def add(k, acc):
            cols = pl.ds(pl.multiple_of(k * DEPTH, DEPTH), DEPTH)
            return acc + dot(xr[a, gam, :, :, cols].reshape(ROWS, DEPTH), wgu[cols, :])
        return lax.fori_loop(0, D // DEPTH, add, jnp.zeros((ROWS, 2 * FF), F32))

    def y_copy(st, gam, d):
        return remote(
            ys.at[st, gam, d - 1], yr.at[st, gam, pl.ds(SLOTS * d, SLOTS)],
            yss.at[st, gam, d - 1], yrs.at[st, gam, d - 1], dev(-d, 0),
        )

    def yp_copy(gam, d):
        return remote(
            yps.at[gam, d - 1], ypr.at[gam, pl.ds(SLOTS * d, SLOTS)],
            ypss.at[gam, d - 1], yprs.at[gam, d - 1], dev(-d, 0),
        )

    def send_back(ab, gam, left, product):
        for c in range(NC):
            st = NC * ab + c
            @pl.loop(0, DC // STEP)
            def _(n, c=c, st=st):
                col = pl.multiple_of(n * STEP, STEP)
                got = product(left, pl.ds(c * DC + col, STEP)).astype(BF16)
                yr[st, gam, pl.ds(0, SLOTS), pl.ds(col, STEP)] = got[:SLOTS]
                for d in range(1, NX):
                    ys[st, gam, d - 1, :, pl.ds(col, STEP)] = got[SLOTS * d : SLOTS * (d + 1)]
            for d in (2, 1, 3):
                y_copy(st, gam, d).start()

    def expert_backward(gam):
        uv = uvb[gam]
        u, v = uv[:, :FF], uv[:, FF:]
        def add(k, acc):
            cols = pl.ds(pl.multiple_of(k * DEPTH, DEPTH), DEPTH)
            return acc + dot_nt(xr[1, gam, :, :, cols].reshape(ROWS, DEPTH), wdv[:, cols])
        q = lax.fori_loop(0, D // DEPTH, add, jnp.zeros((ROWS, FF), F32))
        sig = sigmoid(u)
        act = (u * sig * v).astype(BF16)
        p = jnp.sum(act.astype(F32) * q, axis=1, keepdims=True)
        du = (q * v * sig * (1.0 + u * (1.0 - sig))).astype(BF16)
        dv = (q * u * sig).astype(BF16)
        own = lax.broadcasted_iota(jnp.int32, (ROWS, LANES), 1) == 2 * x + half
        pw = jnp.where(own, p, 0.0).astype(BF16)
        ypr[gam, pl.ds(0, SLOTS), :] = pw[:SLOTS]
        for d in range(1, NX):
            yps[gam, d - 1] = pw[SLOTS * d : SLOTS * (d + 1)]
            yp_copy(gam, d).start()
        send_back(0, gam, jnp.concatenate([du, dv], axis=1), lambda left, cols: dot_nt(left, wgu[cols, :]))

    def expert_forward(gam):
        uv = products(2, gam)
        u, v = uv[:, :FF], uv[:, FF:]
        act = (u * sigmoid(u) * v).astype(BF16)
        send_back(1, gam, act, lambda left, cols: dot(left, wdv[:, cols]))

    def combine(ab, gam):
        for c in range(NC):
            st = NC * ab + c
            for d in range(1, NX):
                y_copy(st, gam, d).wait_recv()
            @pl.loop(0, DC // STEP)
            def _(n, st=st):
                cols = pl.ds(pl.multiple_of(n * STEP, STEP), STEP)
                rows = yr[st, gam, :, cols]
                part = dot(thi[ab, gam], rows) + dot(tlo[ab, gam], rows)
                pacc[st, pl.ds(GROUP * gam, GROUP), :, cols] = part.reshape(GROUP, TOK, STEP)
        if ab == 0:
            for d in range(1, NX):
                yp_copy(gam, d).wait_recv()
            pp[pl.ds(GROUP * gam, GROUP)] = dot(tu[0, gam], ypr[gam]).reshape(GROUP, TOK, LANES)

    def ring_copy(st, slot):
        i = slot - 1
        target = dev(0, -1) if slot % 2 == 1 else dev(0, 1)
        if st < 0:
            return remote(rps.at[i], rpr.at[i], rpss.at[i], rprs.at[i], target)
        return remote(rss.at[st, i], rsr.at[st, i], rsss.at[st, i], rsrs.at[st, i], target)

    def ring_sum(streams, slots):
        for slot in slots:
            for st in streams:
                val = pp[slot] if st < 0 else pacc[st, slot]
                if slot + 2 < NZ:
                    ring_copy(st, slot + 2).wait_recv()
                    val = val + (rpr[slot + 1] if st < 0 else rsr[st, slot + 1]).astype(F32)
                if st < 0:
                    rps[slot - 1] = val.astype(BF16)
                else:
                    rss[st, slot - 1] = val.astype(BF16)
                ring_copy(st, slot).start()

    def ring_result(st):
        for slot in (1, 2):
            ring_copy(st, slot).wait_recv()
        if st < 0:
            return pp[0] + rpr[0].astype(F32) + rpr[1].astype(F32)
        return pacc[st, 0] + rsr[st, 0].astype(F32) + rsr[st, 1].astype(F32)

    for k in range(1, 5):
        z_step(0, k)
    table(0, 0)
    select(0, 0)
    for k in range(5, 9):
        z_step(0, k)
        if k == 6:
            z_start(1)
    table(0, 1)
    select(0, 1)
    for k in range(1, 5):
        z_step(1, k)
    select(1, 0)
    table(1, 0)
    table(1, 1)
    shift.wait_recv()
    _, _, hf = normalize(rx[...])
    for c in range(NC):
        zb[2, c, 0] = hf[:, c * DC : (c + 1) * DC]
    for k in range(5, 9):
        z_step(1, k)
        if k == 6:
            z_start(2)
    select(1, 1)
    for k in range(1, 5):
        z_step(2, k)
    select(2, 0)
    for k in range(5, 9):
        z_step(2, k)
    select(2, 1)

    for load in loads:
        load.wait()
    for gam in range(2):
        gates(0, gam)
        gates(1, gam)
    for gam in range(2):
        x_wait(0, gam)
        uvb[gam] = products(0, gam)
    for gam in range(2):
        x_wait(1, gam)
        expert_backward(gam)
    for gam in range(2):
        x_wait(2, gam)
        expert_forward(gam)

    back = [0, 1, -1]
    combine(0, 1)
    ring_sum(back, range(15, 7, -1))
    combine(0, 0)
    ring_sum(back, range(7, 0, -1))
    dots = ring_result(-1)
    xb, rb, hown = normalize(bx_ref[...])
    mask0 = zm[0].astype(F32)
    logits = dot_nt(hown, cpad[...])
    inside, aff, denom, share = gates_of(logits, mask0, 0, lane16)
    scaled = ROUTE_SCALE * dots
    centre = jnp.sum(jnp.where(inside, share * scaled, 0.0), axis=1, keepdims=True)
    slope = jnp.where(inside, (scaled - centre) / denom * aff * (1.0 - aff), 0.0)
    s1 = slope.astype(BF16)
    s2f = slope - s1.astype(F32)
    s2 = s2f.astype(BF16)
    s3 = (s2f - s2.astype(F32)).astype(BF16)
    dh = jnp.concatenate([ring_result(0), ring_result(1)], axis=1) * ROUTE_SCALE
    dh = dh + dot(s1, cpad[...]) + (dot(s2, cpad[...]) + dot(s3, cpad[...]))
    proj = jnp.sum(dh * xb, axis=1, keepdims=True) * (1.0 / D)
    outb_ref[...] = (dy_ref[...].astype(F32) + rb * dh - rb * rb * rb * xb * proj).astype(BF16)

    front = [2, 3]
    combine(1, 1)
    ring_sum(front, range(15, 7, -1))
    combine(1, 0)
    ring_sum(front, range(7, 0, -1))
    for c in range(NC):
        cols = pl.ds(c * DC, DC)
        outf_ref[:, cols] = (rx[:, cols].astype(F32) + ROUTE_SCALE * ring_result(NC + c)).astype(BF16)

    shift.wait_send()
    for slot in range(1, NZ):
        for a in range(3):
            for piece in pieces(a):
                z_copy(*piece, slot).wait_send()
        for st in range(-1, 2 * NC):
            ring_copy(st, slot).wait_send()
    for gam in range(2):
        for d in range(1, NX):
            for a in range(3):
                x_copy(a, gam, d).wait_send()
            for st in range(2 * NC):
                y_copy(st, gam, d).wait_send()
            yp_copy(gam, d).wait_send()


def on_device(fwd_input, fwd_ids, bwd_input, bwd_ids, bwd_cot, centroids, w_gate, w_up, w_down):
    D = fwd_input.shape[-1]
    DC = D // NC
    FF = w_gate.shape[-1]
    vmem = pl.BlockSpec(memory_space=pltpu.VMEM)
    anym = pl.BlockSpec(memory_space=pl.ANY)
    DMA = pltpu.SemaphoreType.DMA
    V = pltpu.VMEM
    outs = pl.pallas_call(
        kernel,
        out_shape=[jax.ShapeDtypeStruct((TOK, D), BF16)] * 2,
        in_specs=[vmem] * 6 + [anym] * 3,
        out_specs=[vmem] * 2,
        scratch_shapes=[
            V((D, 2 * FF), BF16),
            V((FF, D), BF16),
            V((LANES, D), BF16),
            V((TOK, D), BF16),
            V((NZ, TOK, LANES), BF16),
            V((3, NC, NZ, TOK, DC), BF16),
            V((2, 2, ROWS, GT), BF16),
            V((2, 2, GT, 256), BF16),
            V((2, 2, GT, 256), BF16),
            V((2, 2, GT, 256), BF16),
            V((3, 2, NX - 1, SLOTS, D), BF16),
            V((3, 2, NX, SLOTS, D), BF16),
            V((2 * NC, 2, 256, DC), BF16),
            V((2 * NC, 2, NX - 1, SLOTS, DC), BF16),
            V((2, 256, LANES), BF16),
            V((2, NX - 1, SLOTS, LANES), BF16),
            V((2 * NC, NZ, TOK, DC), F32),
            V((NZ, TOK, LANES), F32),
            V((2 * NC, NZ - 1, TOK, DC), BF16),
            V((2 * NC, NZ - 1, TOK, DC), BF16),
            V((NZ - 1, TOK, LANES), BF16),
            V((NZ - 1, TOK, LANES), BF16),
            V((2, ROWS, 2 * FF), F32),
            DMA((3,)),
            DMA,
            DMA,
            DMA((NZ - 1,)),
            DMA((NZ - 1,)),
            DMA((3, NC, NZ - 1)),
            DMA((3, NC, NZ - 1)),
            DMA((3, 2, NX - 1)),
            DMA((3, 2, NX - 1)),
            DMA((2 * NC, 2, NX - 1)),
            DMA((2 * NC, 2, NX - 1)),
            DMA((2, NX - 1)),
            DMA((2, NX - 1)),
            DMA((2 * NC, NZ - 1)),
            DMA((2 * NC, NZ - 1)),
            DMA((NZ - 1,)),
            DMA((NZ - 1,)),
        ],
        compiler_params=pltpu.CompilerParams(
            collective_id=0, has_side_effects=True, vmem_limit_bytes=60 * 2**20
        ),
        cost_estimate=pl.CostEstimate(flops=6 * 10**9, bytes_accessed=4 * 10**6, transcendentals=0),
        name="expert_layer",
    )(
        fwd_input[0], fwd_ids[0], bwd_input[0], bwd_ids[0], bwd_cot[0], centroids[0],
        w_gate[0], w_up[0], w_down[0],
    )
    return outs[0][None], outs[1][None]


def solution(mesh):
    return jax.shard_map(
        on_device,
        mesh=mesh,
        in_specs=(
            P("section", "expert", None),
            P("section", "expert", None),
            P("section", "expert", None),
            P("section", "expert", None),
            P("section", "expert", None),
            P("section", None, None),
            P("section", None, "expert"),
            P("section", None, "expert"),
            P("section", "expert", None),
        ),
        out_specs=(P("section", "expert", None), P("section", "expert", None)),
        check_vma=False,
    )
```

time: 925 us -> 234 us (0.25)
  waiting for transfers between devices: 793 us -> 0 us
  Pallas kernels: 0 us -> 227 us
  starting transfers between devices: 55.3 us -> 0 us
  local copies, waits for them, and re-layouts: 37.1 us -> 4.27 us
  matrix products: 24.3 us -> 0 us
  other arithmetic: 12.5 us -> 0 us
    all_to_all x6 -> x0, waiting for transfers between devices: 790 us -> none  [the longest x1 165 us: on_device(): lax.all_to_all(sent_normed, 'expert', split_axis=0, concat_axis=0, tiled=...]
    pallas_call x0 -> x1, Pallas kernels: none -> 227 us  [on_device(): pl.pallas_call(kernel, out_shape=[jax.ShapeDtypeStruct((TOK, D), BF16)] *...]
    all_to_all x6 -> x0, starting transfers between devices: 55.2 us -> none  [the longest x1 18.9 us: on_device(): lax.all_to_all(sent_normed, 'expert', split_axis=0, concat_axis=0, tiled=...]
    reshape x8 -> x0, local copies, waits for them, and re-layouts: 27.7 us -> none  [the longest x1 5.57 us: on_device(): rows_normed.reshape(-1, feature_width)]
    dot_general x16 -> x0, matrix products: 24.3 us -> none  [the longest x3 6.35 us: contract_cols(): lax.dot_general(left, right, (((1,), (1,)), ((), ())), preferred_element_...]
    reduce_sum x15 -> x0, other arithmetic: 9.52 us -> none  [the longest x1 2.86 us: on_device(): jnp.sum(back_grads.reshape(EF, shards, CAP, feature_width), axis=1, dtype...]
  transfers between devices with their start and end apart: 7 -> 0, of which waited for: 7 -> 0; matrix products, arithmetic and copies ran while one was open for 5% -> 0% of each run, Pallas kernels for 0% -> 0%
where the time goes in v1:
time: 234 us; the launch traced here: 232 us
  Pallas kernels  227 us (97%)
  local copies, waits for them, and re-layouts  4.27 us (2%)
    pallas_call x1, Pallas kernels, on_device(): pl.pallas_call(kernel, out_shape=[jax.ShapeDtypeStruct((TOK, D), BF16)] *...  227 us

profile of v1, /device:TPU:24, one launch (start us, length us, event | category | flops | bytes accessed | tf_op | source)
XLA Modules:
  0.0 232.4 jit_solution(1864056633279893521)
XLA Ops:
  0.6 0.0 copy-start.1
  0.6 0.7 copy-done.1
  1.3 0.0 copy-start.2
  1.3 0.7 copy.11.fid_ref
  2.0 0.0 copy-done.2
  2.0 0.7 copy.12.bid_ref
  2.7 227.4 %expert_layer.1 = (bf16[16,3584]{1,0:T(8,128)(2,1)}, bf16[16,3584]{1,0:T(8,128)(2,1)}) custom-call(bf16[16,3584]{1,0:T(8,128)(2,1)} %bitcast.18, s32[16,2]{1,0:T(8,128)} %copy.11.fid_ref, bf16[16,3584]{1,0:T(8,128)(2,1)} %bitcast.19, s32[16,2]{1,0:T(8,128)} %copy.12.bid_ref, bf16[16,3584]{1,0:T(8,128)(2,1)} %bitcast.20, bf16[8,3584]{1,0:T(8,128)(2,1)} %bitcast.21, ...), custom_call_target="tpu_custom_call" | custom-call | flops 6000000000 | bytes 4000000 | tf_op jit(solution)/shard_map/expert_layer/pallas_call | solution.py:409
  230.1 0.0 copy-start
  230.1 1.6 copy.15
  231.7 0.0 copy-done
  231.7 0.6 copy.16
Async XLA Ops:
  0.6 0.7 copy-start.1
  1.3 0.7 copy-start.2
  230.1 1.6 copy-start

commit v2 on v1

--- a/solution.py
+++ b/solution.py
@@ -22,7 +22,6 @@
 GT = GROUP * TOK
 LANES = 128
 STEP = 256
-DEPTH = 512
 F32 = jnp.float32
 BF16 = jnp.bfloat16
 NT = (((1,), (1,)), ((), ()))
@@ -43,11 +42,14 @@
 def kernel(
     fx_ref, fid_ref, bx_ref, bid_ref, dy_ref, cent_ref, wg_ref, wu_ref, wd_ref,
     outf_ref, outb_ref,
-    wgu, wdv, cpad, rx, zm, zb, tt, tu, thi, tlo, xs, xr, yr, ys, ypr, yps, pacc, pp, rss, rsr, rps, rpr, uvb,
-    wsem, shs, shr, zms, zmr, zs, zr, xss, xrs, yss, yrs, ypss, yprs, rsss, rsrs, rpss, rprs,
+    wgu, wdv, cpad, rx, zm, zb, tt, tu, thi, tlo, xs, xr, xps, xpr, yr, ys, ypart, ymate, ysum, ypr2, ypr, yps,
+    pacc, pp, rss, rsr, rps, rpr, uvb,
+    wsem, shs, shr, zms, zmr, zs, zr, xss, xrs, xpss, xprs, rls, rlr, yss, yrs, yms, ymr, yus, yur, ypss, yprs,
+    rsss, rsrs, rpss, rprs,
 ):
     D = fx_ref.shape[-1]
     DC = D // NC
+    W = DC // 2
     FF = wdv.shape[0]
     sec = lax.axis_index("section")
     nsec = lax.axis_size("section")
@@ -55,6 +57,8 @@
     x = pos_e // NZ
     z = lax.rem(pos_e, NZ)
     half = z // GROUP
+    par = lax.rem(z, 2)
+    mate_step = 1 - 2 * par
 
     def dev(dx, dz, ds=0):
         xx = lax.rem(x + dx + NX, NX)
@@ -96,12 +100,16 @@
 
     pl.semaphore_wait(barrier, len(partners))
 
+    def place_of(slot, parity):
+        return 8 - parity if slot == 7 else 7 + parity if slot == 8 else slot
+
     def z_copy(a, c, slot):
-        src = 0 if slot <= 2 else slot - 2
+        src = 0 if slot <= 2 else place_of(slot - 2, par)
+        dst = place_of(slot, 1 - par)
         target = dev(0, 1) if slot % 2 == 1 else dev(0, -1)
         if a < 0:
-            return remote(zm.at[src], zm.at[slot], zms.at[slot - 1], zmr.at[slot - 1], target)
-        return remote(zb.at[a, c, src], zb.at[a, c, slot], zs.at[a, c, slot - 1], zr.at[a, c, slot - 1], target)
+            return remote(zm.at[src], zm.at[dst], zms.at[slot - 1], zmr.at[slot - 1], target)
+        return remote(zb.at[a, c, src], zb.at[a, c, dst], zs.at[a, c, slot - 1], zr.at[a, c, slot - 1], target)
 
     def pieces(a):
         return [(-1, 0), (0, 0), (0, 1)] if a == 0 else [(a, c) for c in range(NC)]
@@ -125,13 +133,20 @@
 
     cpad[...] = jnp.zeros_like(cpad)
     cpad[pl.ds(0, 2 * EF), :] = jnp.concatenate([cent_ref[...], cent_ref[...]], axis=0)
-    for st in range(2 * NC):
+    for ab in range(2):
         for gam in range(2):
-            yr[st, gam, pl.ds(ROWS, 256 - ROWS), :] = jnp.zeros((256 - ROWS, DC), BF16)
+            yr[ab, gam, pl.ds(ROWS, 256 - ROWS), :] = jnp.zeros((256 - ROWS, DC), BF16)
+            ypr2[ab, gam, par, pl.ds(ROWS, 256 - ROWS), :] = jnp.zeros((256 - ROWS, W), BF16)
+            ypr2[ab, gam, 1 - par, pl.ds(SLOTS, 256 - SLOTS), :] = jnp.zeros((256 - SLOTS, W), BF16)
     for gam in range(2):
         ypr[gam, pl.ds(ROWS, 256 - ROWS), :] = jnp.zeros((256 - ROWS, LANES), BF16)
 
     lane = lax.broadcasted_iota(jnp.int32, (GT, LANES), 1)
+
+    def away(place, parity):
+        if place in (7, 8):
+            return -4 if (place == 7) == (parity == 1) else 4
+        return place // 2 if place % 2 == 0 else -(place + 1) // 2
 
     def table(ab, gam):
         mask = zm[pl.ds(GROUP * gam, GROUP)].reshape(GT, LANES)
@@ -140,7 +155,12 @@
         below = jnp.where((row_i // TOK == col_i // TOK) & (col_i < row_i), 1.0, 0.0).astype(BF16)
         place = dot(below, mask)
         maskf = mask.astype(F32)
-        base = (lax.broadcasted_iota(jnp.int32, (GT, 1), 0) // TOK * CAP).astype(F32)
+        block = lax.broadcasted_iota(jnp.int32, (GT, 1), 0) // TOK
+        order = jnp.zeros((GT, 1), jnp.int32)
+        for b in range(GROUP):
+            even, odd = [(away(b + GROUP * gam, parity) + parity + 3 - GROUP * gam) % NZ for parity in (0, 1)]
+            order = jnp.where(block == b, even + (odd - even) * par, order)
+        base = (order * CAP).astype(F32)
         wide_lane = lax.broadcasted_iota(jnp.int32, (GT, 256), 1).astype(F32)
         total = jnp.zeros((GT, 256), F32)
         for d in range(NX):
@@ -186,35 +206,81 @@
             xs.at[a, gam, d - 1], xr.at[a, gam, d], xss.at[a, gam, d - 1], xrs.at[a, gam, d - 1], dev(d, 0)
         )
 
-    def select(a, gam):
+    def xp_copy(a, gam, d):
+        return remote(
+            xps.at[a, gam, d - 1], xpr.at[a, gam, par, d], xpss.at[a, gam, d - 1], xprs.at[a, gam, d - 1], dev(d, 0)
+        )
+
+    def relay_copy(a, gam):
+        part = xpr.at[a, gam, par, pl.ds(1, NX - 1)]
+        return remote(part, part, rls.at[a, gam], rlr.at[a, gam], dev(0, mate_step))
+
+    def tokens(a, c, gam, cols):
+        return zb[a, c, pl.ds(GROUP * gam, GROUP), :, cols].reshape(GT, -1)
+
+    def select(a, gam, before=None):
         ab = a // 2
-        for c in range(NC):
-            @pl.loop(0, DC // STEP)
-            def _(n, c=c):
-                col = pl.multiple_of(n * STEP, STEP)
-                rows = zb[a, c, pl.ds(GROUP * gam, GROUP), :, pl.ds(col, STEP)].reshape(GT, STEP)
-                got = dot(tt[ab, gam], rows).astype(BF16)
-                out = pl.ds(c * DC + col, STEP)
-                xr[a, gam, 0, :, out] = got[:SLOTS]
-                for d in range(1, NX):
-                    xs[a, gam, d - 1, :, out] = got[SLOTS * d : SLOTS * (d + 1)]
+        got = dot(tt[ab, gam, pl.ds(SLOTS, ROWS - SLOTS), :],
+                  tokens(a, 0, gam, pl.ds(pl.multiple_of(par * W, LANES), W))).astype(BF16)
+        for d in range(1, NX):
+            xps[a, gam, d - 1] = got[SLOTS * (d - 1) : SLOTS * d]
+        if before is not None:
+            x_sent(*before)
+        for d in (2, 1, 3):
+            xp_copy(a, gam, d).start()
+        for h in range(2):
+            cols = pl.ds(h * W, W)
+            got = dot(tt[ab, gam], tokens(a, 1, gam, cols)).astype(BF16)
+            xr[a, gam, 0, :, cols] = got[:SLOTS]
+            for d in range(1, NX):
+                xs[a, gam, d - 1, :, cols] = got[SLOTS * d : SLOTS * (d + 1)]
         for d in (2, 1, 3):
             x_copy(a, gam, d).start()
+        for h in range(2):
+            got = dot(tt[ab, gam, pl.ds(0, SLOTS), :], tokens(a, 0, gam, pl.ds(h * W, W)))
+            xpr[a, gam, h, 0] = got.astype(BF16)
+
+    def x_sent(a, gam):
+        for d in range(1, NX):
+            xp_copy(a, gam, d).wait_send()
+            x_copy(a, gam, d).wait_send()
+
+    def relay(a, gam):
+        for d in range(1, NX):
+            xp_copy(a, gam, d).wait_recv()
+        relay_copy(a, gam).start()
 
     def x_wait(a, gam):
         for d in range(1, NX):
             x_copy(a, gam, d).wait_recv()
+        relay_copy(a, gam).wait_recv()
+
+    def rows_of(a, gam, j):
+        if j < 2:
+            return xpr[a, gam, j].reshape(ROWS, W)
+        return xr[a, gam, :, :, pl.ds((j - 2) * W, W)].reshape(ROWS, W)
 
     def products(a, gam):
-        def add(k, acc):
-            cols = pl.ds(pl.multiple_of(k * DEPTH, DEPTH), DEPTH)
-            return acc + dot(xr[a, gam, :, :, cols].reshape(ROWS, DEPTH), wgu[cols, :])
-        return lax.fori_loop(0, D // DEPTH, add, jnp.zeros((ROWS, 2 * FF), F32))
-
-    def y_copy(st, gam, d):
+        acc = jnp.zeros((ROWS, 2 * FF), F32)
+        for j in range(4):
+            acc = acc + dot(rows_of(a, gam, j), wgu[pl.ds(j * W, W), :])
+        return acc
+
+    def y_copy(ab, gam, d):
         return remote(
-            ys.at[st, gam, d - 1], yr.at[st, gam, pl.ds(SLOTS * d, SLOTS)],
-            yss.at[st, gam, d - 1], yrs.at[st, gam, d - 1], dev(-d, 0),
+            ys.at[ab, gam, d - 1], yr.at[ab, gam, pl.ds(SLOTS * d, SLOTS)],
+            yss.at[ab, gam, d - 1], yrs.at[ab, gam, d - 1], dev(-d, 0),
+        )
+
+    def mate_copy(ab, gam):
+        return remote(
+            ypart.at[ab, gam, 1 - par], ymate.at[ab, gam], yms.at[ab, gam], ymr.at[ab, gam], dev(0, mate_step)
+        )
+
+    def ysum_copy(ab, gam, d):
+        return remote(
+            ysum.at[ab, gam, d - 1], ypr2.at[ab, gam, par, pl.ds(SLOTS * d, SLOTS)],
+            yus.at[ab, gam, d - 1], yur.at[ab, gam, d - 1], dev(-d, 0),
         )
 
     def yp_copy(gam, d):
@@ -224,25 +290,43 @@
         )
 
     def send_back(ab, gam, left, product):
-        for c in range(NC):
-            st = NC * ab + c
-            @pl.loop(0, DC // STEP)
-            def _(n, c=c, st=st):
-                col = pl.multiple_of(n * STEP, STEP)
-                got = product(left, pl.ds(c * DC + col, STEP)).astype(BF16)
-                yr[st, gam, pl.ds(0, SLOTS), pl.ds(col, STEP)] = got[:SLOTS]
+        for j in range(4):
+            got = product(left, pl.ds(j * W, W)).astype(BF16)
+            if j < 2:
+                ypr2[ab, gam, j, pl.ds(0, SLOTS), :] = got[:SLOTS]
                 for d in range(1, NX):
-                    ys[st, gam, d - 1, :, pl.ds(col, STEP)] = got[SLOTS * d : SLOTS * (d + 1)]
-            for d in (2, 1, 3):
-                y_copy(st, gam, d).start()
+                    ypart[ab, gam, j, d - 1] = got[SLOTS * d : SLOTS * (d + 1)]
+                if j == 1:
+                    mate_copy(ab, gam).start()
+            else:
+                cols = pl.ds((j - 2) * W, W)
+                yr[ab, gam, pl.ds(0, SLOTS), cols] = got[:SLOTS]
+                for d in range(1, NX):
+                    ys[ab, gam, d - 1, :, cols] = got[SLOTS * d : SLOTS * (d + 1)]
+
+    def y_start(ab, gam):
+        for d in (2, 1, 3):
+            y_copy(ab, gam, d).start()
+
+    def pair_start(ab, gam):
+        mate_copy(ab, gam).wait_recv()
+        for d in (2, 1, 3):
+            both = ypart[ab, gam, par, d - 1].astype(F32) + ymate[ab, gam, d - 1].astype(F32)
+            ysum[ab, gam, d - 1] = both.astype(BF16)
+            ysum_copy(ab, gam, d).start()
+
+    def y_sent(ab, gam):
+        mate_copy(ab, gam).wait_send()
+        for d in range(1, NX):
+            y_copy(ab, gam, d).wait_send()
+            ysum_copy(ab, gam, d).wait_send()
 
     def expert_backward(gam):
         uv = uvb[gam]
         u, v = uv[:, :FF], uv[:, FF:]
-        def add(k, acc):
-            cols = pl.ds(pl.multiple_of(k * DEPTH, DEPTH), DEPTH)
-            return acc + dot_nt(xr[1, gam, :, :, cols].reshape(ROWS, DEPTH), wdv[:, cols])
-        q = lax.fori_loop(0, D // DEPTH, add, jnp.zeros((ROWS, FF), F32))
+        q = jnp.zeros((ROWS, FF), F32)
+        for j in range(4):
+            q = q + dot_nt(rows_of(1, gam, j), wdv[:, pl.ds(j * W, W)])
         sig = sigmoid(u)
         act = (u * sig * v).astype(BF16)
         p = jnp.sum(act.astype(F32) * q, axis=1, keepdims=True)
@@ -263,16 +347,14 @@
         send_back(1, gam, act, lambda left, cols: dot(left, wdv[:, cols]))
 
     def combine(ab, gam):
-        for c in range(NC):
-            st = NC * ab + c
-            for d in range(1, NX):
-                y_copy(st, gam, d).wait_recv()
-            @pl.loop(0, DC // STEP)
-            def _(n, st=st):
-                cols = pl.ds(pl.multiple_of(n * STEP, STEP), STEP)
-                rows = yr[st, gam, :, cols]
-                part = dot(thi[ab, gam], rows) + dot(tlo[ab, gam], rows)
-                pacc[st, pl.ds(GROUP * gam, GROUP), :, cols] = part.reshape(GROUP, TOK, STEP)
+        for d in range(1, NX):
+            y_copy(ab, gam, d).wait_recv()
+            ysum_copy(ab, gam, d).wait_recv()
+        for j in range(4):
+            cols = pl.ds((j % 2) * W, W)
+            rows = ypr2[ab, gam, j] if j < 2 else yr[ab, gam, :, cols]
+            part = dot(thi[ab, gam], rows) + dot(tlo[ab, gam], rows)
+            pacc[NC * ab + j // 2, pl.ds(GROUP * gam, GROUP), :, cols] = part.reshape(GROUP, TOK, W)
         if ab == 0:
             for d in range(1, NX):
                 yp_copy(gam, d).wait_recv()
@@ -288,7 +370,8 @@
     def ring_sum(streams, slots):
         for slot in slots:
             for st in streams:
-                val = pp[slot] if st < 0 else pacc[st, slot]
+                place = place_of(slot, par)
+                val = pp[place] if st < 0 else pacc[st, place]
                 if slot + 2 < NZ:
                     ring_copy(st, slot + 2).wait_recv()
                     val = val + (rpr[slot + 1] if st < 0 else rsr[st, slot + 1]).astype(F32)
@@ -307,55 +390,66 @@
 
     for k in range(1, 5):
         z_step(0, k)
+    z_start(1)
     table(0, 0)
     select(0, 0)
-    for k in range(5, 9):
-        z_step(0, k)
-        if k == 6:
-            z_start(1)
-    table(0, 1)
-    select(0, 1)
-    for k in range(1, 5):
-        z_step(1, k)
-    select(1, 0)
-    table(1, 0)
-    table(1, 1)
     shift.wait_recv()
     _, _, hf = normalize(rx[...])
     for c in range(NC):
         zb[2, c, 0] = hf[:, c * DC : (c + 1) * DC]
-    for k in range(5, 9):
+    for k in range(1, 5):
+        z_step(0, k + 4)
         z_step(1, k)
-        if k == 6:
-            z_start(2)
+    z_start(2)
+    table(0, 1)
+    select(0, 1)
+    select(1, 0)
+    relay(0, 0)
+    for k in range(1, 5):
+        z_step(1, k + 4)
+        z_step(2, k)
+    table(1, 0)
+    table(1, 1)
     select(1, 1)
-    for k in range(1, 5):
-        z_step(2, k)
     select(2, 0)
+    relay(0, 1)
+    relay(1, 0)
     for k in range(5, 9):
         z_step(2, k)
     select(2, 1)
+    relay(1, 1)
 
     for load in loads:
         load.wait()
-    for gam in range(2):
+    for gam in (0, 1):
         gates(0, gam)
-        gates(1, gam)
-    for gam in range(2):
         x_wait(0, gam)
         uvb[gam] = products(0, gam)
-    for gam in range(2):
+    relay(2, 0)
+    for gam in (1, 0):
         x_wait(1, gam)
         expert_backward(gam)
-    for gam in range(2):
+        y_start(0, gam)
+    relay(2, 1)
+    pair_start(0, 1)
+    pair_start(0, 0)
+    for gam in (1, 0):
+        gates(1, gam)
         x_wait(2, gam)
         expert_forward(gam)
-
+        y_start(1, gam)
+    pair_start(1, 1)
+    pair_start(1, 0)
     back = [0, 1, -1]
+    front = [2, 3]
     combine(0, 1)
-    ring_sum(back, range(15, 7, -1))
+    ring_sum(back, range(15, 8, -1))
     combine(0, 0)
-    ring_sum(back, range(7, 0, -1))
+    combine(1, 1)
+    for slot in range(7, 0, -1):
+        ring_sum(back, [slot + 1])
+        ring_sum(front, [slot + 8])
+    ring_sum(back, [1])
     dots = ring_result(-1)
     xb, rb, hown = normalize(bx_ref[...])
     mask0 = zm[0].astype(F32)
@@ -373,11 +467,8 @@
     proj = jnp.sum(dh * xb, axis=1, keepdims=True) * (1.0 / D)
     outb_ref[...] = (dy_ref[...].astype(F32) + rb * dh - rb * rb * rb * xb * proj).astype(BF16)
 
-    front = [2, 3]
-    combine(1, 1)
-    ring_sum(front, range(15, 7, -1))
     combine(1, 0)
-    ring_sum(front, range(7, 0, -1))
+    ring_sum(front, range(8, 0, -1))
     for c in range(NC):
         cols = pl.ds(c * DC, DC)
         outf_ref[:, cols] = (rx[:, cols].astype(F32) + ROUTE_SCALE * ring_result(NC + c)).astype(BF16)
@@ -390,17 +481,19 @@
         for st in range(-1, 2 * NC):
             ring_copy(st, slot).wait_send()
     for gam in range(2):
-        for d in range(1, NX):
-            for a in range(3):
-                x_copy(a, gam, d).wait_send()
-            for st in range(2 * NC):
-                y_copy(st, gam, d).wait_send()
+        for a in range(3):
+            x_sent(a, gam)
+            relay_copy(a, gam).wait_send()
+        for ab in range(2):
+            y_sent(ab, gam)
+        for d in range(1, NX):
             yp_copy(gam, d).wait_send()
 
 
 def on_device(fwd_input, fwd_ids, bwd_input, bwd_ids, bwd_cot, centroids, w_gate, w_up, w_down):
     D = fwd_input.shape[-1]
     DC = D // NC
+    W = DC // 2
     FF = w_gate.shape[-1]
     vmem = pl.BlockSpec(memory_space=pltpu.VMEM)
     anym = pl.BlockSpec(memory_space=pl.ANY)
@@ -422,10 +515,16 @@
             V((2, 2, GT, 256), BF16),
             V((2, 2, GT, 256), BF16),
             V((2, 2, GT, 256), BF16),
-            V((3, 2, NX - 1, SLOTS, D), BF16),
-            V((3, 2, NX, SLOTS, D), BF16),
-            V((2 * NC, 2, 256, DC), BF16),
-            V((2 * NC, 2, NX - 1, SLOTS, DC), BF16),
+            V((3, 2, NX - 1, SLOTS, DC), BF16),
+            V((3, 2, NX, SLOTS, DC), BF16),
+            V((3, 2, NX - 1, SLOTS, W), BF16),
+            V((3, 2, 2, NX, SLOTS, W), BF16),
+            V((2, 2, 256, DC), BF16),
+            V((2, 2, NX - 1, SLOTS, DC), BF16),
+            V((2, 2, 2, NX - 1, SLOTS, W), BF16),
+            V((2, 2, NX - 1, SLOTS, W), BF16),
+            V((2, 2, NX - 1, SLOTS, W), BF16),
+            V((2, 2, 2, 256, W), BF16),
             V((2, 256, LANES), BF16),
             V((2, NX - 1, SLOTS, LANES), BF16),
             V((2 * NC, NZ, TOK, DC), F32),
@@ -444,8 +543,16 @@
             DMA((3, NC, NZ - 1)),
             DMA((3, 2, NX - 1)),
             DMA((3, 2, NX - 1)),
-            DMA((2 * NC, 2, NX - 1)),
-            DMA((2 * NC, 2, NX - 1)),
+            DMA((3, 2, NX - 1)),
+            DMA((3, 2, NX - 1)),
+            DMA((3, 2)),
+            DMA((3, 2)),
+            DMA((2, 2, NX - 1)),
+            DMA((2, 2, NX - 1)),
+            DMA((2, 2)),
+            DMA((2, 2)),
+            DMA((2, 2, NX - 1)),
+            DMA((2, 2, NX - 1)),
             DMA((2, NX - 1)),
             DMA((2, NX - 1)),
             DMA((2 * NC, NZ - 1)),

time: 234 us -> 205 us (0.88)
  Pallas kernels: 227 us -> 198 us
    pallas_call x1, Pallas kernels: 227 us -> 198 us  [on_device(): pl.pallas_call(kernel, out_shape=[jax.ShapeDtypeStruct((TOK, D), BF16)] *...]
where the time goes in v2:
time: 205 us; the launch traced here: 203 us
  Pallas kernels  198 us (97%)
  local copies, waits for them, and re-layouts  4.27 us (2%)
    pallas_call x1, Pallas kernels, on_device(): pl.pallas_call(kernel, out_shape=[jax.ShapeDtypeStruct((TOK, D), BF16)] *...  198 us

profile of v2, /device:TPU:24, one launch (start us, length us, event | category | flops | bytes accessed | tf_op | source)
XLA Modules:
  0.0 202.7 jit_solution(7950770069008727155)
XLA Ops:
  0.6 0.0 copy-start.1
  0.6 0.7 copy-done.1
  1.3 0.0 copy-start.2
  1.3 0.7 copy.11.fid_ref
  2.0 0.0 copy-done.2
  2.0 0.7 copy.12.bid_ref
  2.7 197.8 %expert_layer.1 = (bf16[16,3584]{1,0:T(8,128)(2,1)}, bf16[16,3584]{1,0:T(8,128)(2,1)}) custom-call(bf16[16,3584]{1,0:T(8,128)(2,1)} %bitcast.18, s32[16,2]{1,0:T(8,128)} %copy.11.fid_ref, bf16[16,3584]{1,0:T(8,128)(2,1)} %bitcast.19, s32[16,2]{1,0:T(8,128)} %copy.12.bid_ref, bf16[16,3584]{1,0:T(8,128)(2,1)} %bitcast.20, bf16[8,3584]{1,0:T(8,128)(2,1)} %bitcast.21, ...), custom_call_target="tpu_custom_call" | custom-call | flops 6000000000 | bytes 4000000 | tf_op jit(solution)/shard_map/expert_layer/pallas_call | solution.py:502
  200.5 0.0 copy-start
  200.5 1.6 copy.15
  202.1 0.0 copy-done
  202.1 0.6 copy.16
Async XLA Ops:
  0.6 0.7 copy-start.1
  1.3 0.7 copy-start.2
  200.5 1.6 copy-start

commit v3 on v2

--- a/solution.py
+++ b/solution.py
@@ -43,9 +43,9 @@
     fx_ref, fid_ref, bx_ref, bid_ref, dy_ref, cent_ref, wg_ref, wu_ref, wd_ref,
     outf_ref, outb_ref,
     wgu, wdv, cpad, rx, zm, zb, tt, tu, thi, tlo, xs, xr, xps, xpr, yr, ys, ypart, ymate, ysum, ypr2, ypr, yps,
-    pacc, pp, rss, rsr, rps, rpr, uvb,
+    pacc, rss, rsr, uvb, gsh, gco,
     wsem, shs, shr, zms, zmr, zs, zr, xss, xrs, xpss, xprs, rls, rlr, yss, yrs, yms, ymr, yus, yur, ypss, yprs,
-    rsss, rsrs, rpss, rprs,
+    rsss, rsrs,
 ):
     D = fx_ref.shape[-1]
     DC = D // NC
@@ -189,7 +189,10 @@
                 return acc + dot_nt(rows, cpad[:, pl.ds(c * DC + col, STEP)])
             acc = lax.fori_loop(0, DC // STEP, add, acc)
         mask = zm[pl.ds(GROUP * gam, GROUP)].reshape(GT, LANES).astype(F32)
-        _, _, _, share = gates_of(acc, mask, ab, lane)
+        inside, aff, denom, share = gates_of(acc, mask, ab, lane)
+        if ab == 0:
+            gsh[gam] = share
+            gco[gam] = jnp.where(inside, aff * (1.0 - aff) / denom, 0.0)
         block = lax.broadcasted_iota(jnp.int32, (GT, 256), 1) // SLOTS
         spread = jnp.zeros((GT, 256), F32)
         for d in range(NX):
@@ -240,7 +243,12 @@
             got = dot(tt[ab, gam, pl.ds(0, SLOTS), :], tokens(a, 0, gam, pl.ds(h * W, W)))
             xpr[a, gam, h, 0] = got.astype(BF16)
 
+    settled = set()
+
     def x_sent(a, gam):
+        if ("x", a, gam) in settled:
+            return
+        settled.add(("x", a, gam))
         for d in range(1, NX):
             xp_copy(a, gam, d).wait_send()
             x_copy(a, gam, d).wait_send()
@@ -316,6 +324,9 @@
             ysum_copy(ab, gam, d).start()
 
     def y_sent(ab, gam):
+        if ("y", ab, gam) in settled:
+            return
+        settled.add(("y", ab, gam))
         mate_copy(ab, gam).wait_send()
         for d in range(1, NX):
             y_copy(ab, gam, d).wait_send()
@@ -350,42 +361,41 @@
         for d in range(1, NX):
             y_copy(ab, gam, d).wait_recv()
             ysum_copy(ab, gam, d).wait_recv()
+        if ab == 0:
+            for d in range(1, NX):
+                yp_copy(gam, d).wait_recv()
+            dots = dot(tu[0, gam], ypr[gam])
+            centre = jnp.sum(gsh[gam] * dots, axis=1, keepdims=True)
+            slope = (dots - centre) * gco[gam]
+            slope_hi = slope.astype(BF16)
+            slope_lo = (slope - slope_hi.astype(F32)).astype(BF16)
         for j in range(4):
             cols = pl.ds((j % 2) * W, W)
             rows = ypr2[ab, gam, j] if j < 2 else yr[ab, gam, :, cols]
             part = dot(thi[ab, gam], rows) + dot(tlo[ab, gam], rows)
+            if ab == 0:
+                centres = cpad[:, pl.ds(j * W, W)]
+                part = part + dot(slope_hi, centres) + dot(slope_lo, centres)
             pacc[NC * ab + j // 2, pl.ds(GROUP * gam, GROUP), :, cols] = part.reshape(GROUP, TOK, W)
-        if ab == 0:
-            for d in range(1, NX):
-                yp_copy(gam, d).wait_recv()
-            pp[pl.ds(GROUP * gam, GROUP)] = dot(tu[0, gam], ypr[gam]).reshape(GROUP, TOK, LANES)
 
     def ring_copy(st, slot):
         i = slot - 1
         target = dev(0, -1) if slot % 2 == 1 else dev(0, 1)
-        if st < 0:
-            return remote(rps.at[i], rpr.at[i], rpss.at[i], rprs.at[i], target)
         return remote(rss.at[st, i], rsr.at[st, i], rsss.at[st, i], rsrs.at[st, i], target)
 
     def ring_sum(streams, slots):
         for slot in slots:
             for st in streams:
-                place = place_of(slot, par)
-                val = pp[place] if st < 0 else pacc[st, place]
+                val = pacc[st, place_of(slot, par)]
                 if slot + 2 < NZ:
                     ring_copy(st, slot + 2).wait_recv()
-                    val = val + (rpr[slot + 1] if st < 0 else rsr[st, slot + 1]).astype(F32)
-                if st < 0:
-                    rps[slot - 1] = val.astype(BF16)
-                else:
-                    rss[st, slot - 1] = val.astype(BF16)
+                    val = val + rsr[st, slot + 1].astype(F32)
+                rss[st, slot - 1] = val.astype(BF16)
                 ring_copy(st, slot).start()
 
     def ring_result(st):
         for slot in (1, 2):
             ring_copy(st, slot).wait_recv()
-        if st < 0:
-            return pp[0] + rpr[0].astype(F32) + rpr[1].astype(F32)
         return pacc[st, 0] + rsr[st, 0].astype(F32) + rsr[st, 1].astype(F32)
 
     for k in range(1, 5):
@@ -409,11 +419,11 @@
         z_step(1, k + 4)
         z_step(2, k)
     table(1, 0)
-    table(1, 1)
     select(1, 1)
     select(2, 0)
     relay(0, 1)
     relay(1, 0)
+    table(1, 1)
     for k in range(5, 9):
         z_step(2, k)
     select(2, 1)
@@ -422,7 +432,6 @@
     for load in loads:
         load.wait()
     for gam in (0, 1):
-        gates(0, gam)
         x_wait(0, gam)
         uvb[gam] = products(0, gam)
     relay(2, 0)
@@ -430,45 +439,43 @@
         x_wait(1, gam)
         expert_backward(gam)
         y_start(0, gam)
+        if gam == 0:
+            pair_start(0, 1)
     relay(2, 1)
-    pair_start(0, 1)
     pair_start(0, 0)
-    for gam in (1, 0):
-        gates(1, gam)
-        x_wait(2, gam)
-        expert_forward(gam)
-        y_start(1, gam)
+    gates(0, 1)
+    gates(0, 0)
+    x_wait(2, 1)
+    expert_forward(1)
+    y_start(1, 1)
+    x_wait(2, 0)
+    expert_forward(0)
     pair_start(1, 1)
-    pair_start(1, 0)
-    back = [0, 1, -1]
+    y_start(1, 0)
+    back = [0, 1]
     front = [2, 3]
     combine(0, 1)
-    ring_sum(back, range(15, 8, -1))
+    ring_sum(back, range(15, 12, -1))
+    pair_start(1, 0)
+    gates(1, 1)
+    ring_sum(back, range(12, 10, -1))
+    gates(1, 0)
+    ring_sum(back, range(10, 8, -1))
     combine(0, 0)
+    ring_sum(back, range(8, 4, -1))
     combine(1, 1)
-    for slot in range(7, 0, -1):
-        ring_sum(back, [slot + 1])
-        ring_sum(front, [slot + 8])
-    ring_sum(back, [1])
-    dots = ring_result(-1)
-    xb, rb, hown = normalize(bx_ref[...])
-    mask0 = zm[0].astype(F32)
-    logits = dot_nt(hown, cpad[...])
-    inside, aff, denom, share = gates_of(logits, mask0, 0, lane16)
-    scaled = ROUTE_SCALE * dots
-    centre = jnp.sum(jnp.where(inside, share * scaled, 0.0), axis=1, keepdims=True)
-    slope = jnp.where(inside, (scaled - centre) / denom * aff * (1.0 - aff), 0.0)
-    s1 = slope.astype(BF16)
-    s2f = slope - s1.astype(F32)
-    s2 = s2f.astype(BF16)
-    s3 = (s2f - s2.astype(F32)).astype(BF16)
+    for slot in range(4, 0, -1):
+        ring_sum(back, [slot])
+        ring_sum(front, [slot + 11])
+    ring_sum(front, range(11, 8, -1))
+    combine(1, 0)
+    ring_sum(front, range(8, 6, -1))
+    xb, rb, _ = normalize(bx_ref[...])
     dh = jnp.concatenate([ring_result(0), ring_result(1)], axis=1) * ROUTE_SCALE
-    dh = dh + dot(s1, cpad[...]) + (dot(s2, cpad[...]) + dot(s3, cpad[...]))
     proj = jnp.sum(dh * xb, axis=1, keepdims=True) * (1.0 / D)
     outb_ref[...] = (dy_ref[...].astype(F32) + rb * dh - rb * rb * rb * xb * proj).astype(BF16)
 
-    combine(1, 0)
-    ring_sum(front, range(8, 0, -1))
+    ring_sum(front, range(6, 0, -1))
     for c in range(NC):
         cols = pl.ds(c * DC, DC)
         outf_ref[:, cols] = (rx[:, cols].astype(F32) + ROUTE_SCALE * ring_result(NC + c)).astype(BF16)
@@ -478,7 +485,7 @@
         for a in range(3):
             for piece in pieces(a):
                 z_copy(*piece, slot).wait_send()
-        for st in range(-1, 2 * NC):
+        for st in range(2 * NC):
             ring_copy(st, slot).wait_send()
     for gam in range(2):
         for a in range(3):
@@ -528,12 +535,11 @@
             V((2, 256, LANES), BF16),
             V((2, NX - 1, SLOTS, LANES), BF16),
             V((2 * NC, NZ, TOK, DC), F32),
-            V((NZ, TOK, LANES), F32),
             V((2 * NC, NZ - 1, TOK, DC), BF16),
             V((2 * NC, NZ - 1, TOK, DC), BF16),
-            V((NZ - 1, TOK, LANES), BF16),
-            V((NZ - 1, TOK, LANES), BF16),
             V((2, ROWS, 2 * FF), F32),
+            V((2, GT, LANES), F32),
+            V((2, GT, LANES), F32),
             DMA((3,)),
             DMA,
             DMA,
@@ -557,8 +563,6 @@
             DMA((2, NX - 1)),
             DMA((2 * NC, NZ - 1)),
             DMA((2 * NC, NZ - 1)),
-            DMA((NZ - 1,)),
-            DMA((NZ - 1,)),
         ],
         compiler_params=pltpu.CompilerParams(
             collective_id=0, has_side_effects=True, vmem_limit_bytes=60 * 2**20

time: 205 us -> 200 us (0.976)
  Pallas kernels: 198 us -> 193 us
    pallas_call x1, Pallas kernels: 198 us -> 193 us  [on_device(): pl.pallas_call(kernel, out_shape=[jax.ShapeDtypeStruct((TOK, D), BF16)] *...]
where the time goes in v3:
time: 200 us; the launch traced here: 198 us
  Pallas kernels  193 us (96%)
  local copies, waits for them, and re-layouts  4.27 us (2%)
    pallas_call x1, Pallas kernels, on_device(): pl.pallas_call(kernel, out_shape=[jax.ShapeDtypeStruct((TOK, D), BF16)] *...  193 us

profile of v3, /device:TPU:24, one launch (start us, length us, event | category | flops | bytes accessed | tf_op | source)
XLA Modules:
  0.0 198.3 jit_solution(13475850539844582020)
XLA Ops:
  0.6 0.0 copy-start.1
  0.6 0.7 copy-done.1
  1.3 0.0 copy-start.2
  1.3 0.7 copy.11.fid_ref
  2.0 0.0 copy-done.2
  2.0 0.7 copy.12.bid_ref
  2.7 193.4 %expert_layer.1 = (bf16[16,3584]{1,0:T(8,128)(2,1)}, bf16[16,3584]{1,0:T(8,128)(2,1)}) custom-call(bf16[16,3584]{1,0:T(8,128)(2,1)} %bitcast.18, s32[16,2]{1,0:T(8,128)} %copy.11.fid_ref, bf16[16,3584]{1,0:T(8,128)(2,1)} %bitcast.19, s32[16,2]{1,0:T(8,128)} %copy.12.bid_ref, bf16[16,3584]{1,0:T(8,128)(2,1)} %bitcast.20, bf16[8,3584]{1,0:T(8,128)(2,1)} %bitcast.21, ...), custom_call_target="tpu_custom_call" | custom-call | flops 6000000000 | bytes 4000000 | tf_op jit(solution)/shard_map/expert_layer/pallas_call | solution.py:509
  196.1 0.0 copy-start
  196.1 1.6 copy.15
  197.7 0.0 copy-done
  197.7 0.6 copy.16
Async XLA Ops:
  0.6 0.7 copy-start.1
  1.3 0.7 copy-start.2
  196.1 1.6 copy-start

commit v4 on v3

--- a/solution.py
+++ b/solution.py
@@ -455,19 +455,20 @@
     back = [0, 1]
     front = [2, 3]
     combine(0, 1)
-    ring_sum(back, range(15, 12, -1))
+    ring_sum(back, range(15, 14, -1))
     pair_start(1, 0)
+    ring_sum(back, range(14, 12, -1))
     gates(1, 1)
     ring_sum(back, range(12, 10, -1))
     gates(1, 0)
     ring_sum(back, range(10, 8, -1))
     combine(0, 0)
-    ring_sum(back, range(8, 4, -1))
+    ring_sum(back, range(8, 6, -1))
     combine(1, 1)
-    for slot in range(4, 0, -1):
+    ring_sum(front, [15])
+    for slot in range(6, 0, -1):
         ring_sum(back, [slot])
-        ring_sum(front, [slot + 11])
-    ring_sum(front, range(11, 8, -1))
+        ring_sum(front, [slot + 8])
     combine(1, 0)
     ring_sum(front, range(8, 6, -1))
     xb, rb, _ = normalize(bx_ref[...])

time: 200 us -> 196 us (0.980)
  Pallas kernels: 193 us -> 190 us
    pallas_call x1, Pallas kernels: 193 us -> 190 us  [on_device(): pl.pallas_call(kernel, out_shape=[jax.ShapeDtypeStruct((TOK, D), BF16)] *...]
where the time goes in v4:
time: 196 us; the launch traced here: 195 us
  Pallas kernels  190 us (97%)
  local copies, waits for them, and re-layouts  4.27 us (2%)
    pallas_call x1, Pallas kernels, on_device(): pl.pallas_call(kernel, out_shape=[jax.ShapeDtypeStruct((TOK, D), BF16)] *...  190 us

profile of v4, /device:TPU:24, one launch (start us, length us, event | category | flops | bytes accessed | tf_op | source)
XLA Modules:
  0.0 194.5 jit_solution(4248154613172367816)
XLA Ops:
  0.6 0.0 copy-start.1
  0.6 0.7 copy-done.1
  1.3 0.0 copy-start.2
  1.3 0.7 copy.11.fid_ref
  2.0 0.0 copy-done.2
  2.0 0.7 copy.12.bid_ref
  2.7 189.6 %expert_layer.1 = (bf16[16,3584]{1,0:T(8,128)(2,1)}, bf16[16,3584]{1,0:T(8,128)(2,1)}) custom-call(bf16[16,3584]{1,0:T(8,128)(2,1)} %bitcast.18, s32[16,2]{1,0:T(8,128)} %copy.11.fid_ref, bf16[16,3584]{1,0:T(8,128)(2,1)} %bitcast.19, s32[16,2]{1,0:T(8,128)} %copy.12.bid_ref, bf16[16,3584]{1,0:T(8,128)(2,1)} %bitcast.20, bf16[8,3584]{1,0:T(8,128)(2,1)} %bitcast.21, ...), custom_call_target="tpu_custom_call" | custom-call | flops 6000000000 | bytes 4000000 | tf_op jit(solution)/shard_map/expert_layer/pallas_call | solution.py:510
  192.3 0.0 copy-start
  192.3 1.6 copy.15
  193.9 0.0 copy-done
  193.9 0.6 copy.16
Async XLA Ops:
  0.6 0.7 copy-start.1
  1.3 0.7 copy-start.2
  192.3 1.6 copy-start
